TPU v7x, 32 devices: a whole 2x2x4 slice. The times are simulated.
32 devices in a mesh: grid: 2 (over y), wide: 4 (over z), narrow: 4 (over x, core).
Axes of the slice: x: 2, y: 2, z: 4, core: 2. Of those that a mesh axis runs over, the one named last changes fastest.
Arguments:
- tokens: bfloat16 [4096, 8192], P(('grid', 'wide'), 'narrow'), parts along dimension 0, may hold values from -6 to 6
- frozen_value_weight: bfloat16 [8192, 1024], P('narrow'), may hold values from -0.0625 to 0.0625
- token_adapter_index: int32 [4096, 1], P(('grid', 'wide')), parts along dimension 0, may hold values from 0 to 7; in each aligned block of 512 rows (0 to 511, 512 to 1023, ...) at most 192 rows name the same one
- adapter_down_weight: float32 [16384, 128], P(('grid', 'narrow'), 'wide'), parts along dimension 0, may hold values from -0.0625 to 0.0625
- adapter_up_weight: float32 [256, 1024], P(('grid', 'wide'), 'narrow'), parts along dimension 0, may hold values from -0.1875 to 0.1875
- down_moment_first: float32 [16384, 128], P(('grid', 'narrow'), 'wide'), parts along dimension 0, may hold values from -12 to 12
- down_moment_second: float32 [16384, 128], P(('grid', 'narrow'), 'wide'), parts along dimension 0, may hold values from 1 to 100
- up_moment_first: float32 [256, 1024], P(('grid', 'wide'), 'narrow'), parts along dimension 0, may hold values from -12 to 12
- up_moment_second: float32 [256, 1024], P(('grid', 'wide'), 'narrow'), parts along dimension 0, may hold values from 1 to 100
- rates: float32 [16], P(('grid', 'wide')), parts along dimension 0, may hold values from 0.01 to 0.2
- value_output_gradient: bfloat16 [4096, 1024], P(('grid', 'wide', 'narrow')), parts along dimension 0, may hold values from -6 to 6
Outputs:
- values: bfloat16 [4096, 1024], P(('grid', 'wide', 'narrow')), parts along dimension 0
- grad_tokens: bfloat16 [4096, 8192], P(('grid', 'wide'), 'narrow'), parts along dimension 0
- updated_down_weight: float32 [16384, 128], P(('grid', 'narrow'), 'wide'), parts along dimension 0
- updated_down_moment_first: float32 [16384, 128], P(('grid', 'narrow'), 'wide'), parts along dimension 0
- updated_down_moment_second: float32 [16384, 128], P(('grid', 'narrow'), 'wide'), parts along dimension 0
- updated_up_weight: float32 [256, 1024], P(('grid', 'wide'), 'narrow'), parts along dimension 0
- updated_up_moment_first: float32 [256, 1024], P(('grid', 'wide'), 'narrow'), parts along dimension 0
- updated_up_moment_second: float32 [256, 1024], P(('grid', 'wide'), 'narrow'), parts along dimension 0
There are 2 independent parts, one for each index of `grid`. A program takes and returns all parts, laid end to end along the dimension named above; an argument that names none is the same for every part. Nothing has to cross between parts.
Inputs may be any that keep to these rules, and one draw needn't show every extreme that they name: `token_adapter_index`: within the tokens of one index of wide (aligned blocks of 512 rows) no adapter is named by more than 192 rows, and in every draw some adapter is named by exactly 192 rows of some block.
All inputs are finite; a program needn't handle non-finite values.
Results may differ from a plain program's by a relative error of at most 0.009.
Values may be sent and summed in bfloat16 or wider, within the bound.
A program may use at most 64 MiB of HBM per device.

v0:
```python
import jax
import jax.numpy as jnp
from jax import lax
from jax.sharding import PartitionSpec as P

ADAPTER_RANK = 16
STEP = 1000


adapter_scale = 2.0
beta_first = 0.9
beta_second = 0.999
adam_eps = 1e-08


def expand_codes(lowrank, selector):
    item_count = lowrank.shape[0]
    return (selector[:, :, None] * lowrank[:, None, :]).reshape(item_count, -1)


def packed_adapter_index(spread, selector):
    item_count = spread.shape[0]
    return jnp.sum(spread.reshape(item_count, selector.shape[1], -1) * selector[:, :, None], axis=1)


def apply_adam_moments(parameter, first, second, gradient, step_rate):
    first_new = beta_first * first + (1.0 - beta_first) * gradient
    second_new = beta_second * second + (1.0 - beta_second) * gradient * gradient
    first_fix = 1.0 - beta_first**STEP
    second_fix = 1.0 - beta_second**STEP
    update = step_rate * (first_new / first_fix) / (jnp.sqrt(second_new / second_fix) + adam_eps)
    return (parameter - update, first_new, second_new)


def shards(
    tokens,
    frozen_value_weight,
    token_adapter_index,
    adapter_down_weight,
    adapter_up_weight,
    down_moment_first,
    down_moment_second,
    up_moment_first,
    up_moment_second,
    rates,
    value_output_gradient,
):
    wide_adapter_count = lax.axis_size("wide")
    narrow_count = lax.axis_size("narrow")
    narrow_index = lax.axis_index("narrow")
    token_count = tokens.shape[0]
    row_count = token_count // narrow_count
    row_start = narrow_index * row_count
    adapter_members = adapter_down_weight.shape[1] * wide_adapter_count // ADAPTER_RANK
    selector = token_adapter_index == jnp.arange(adapter_members, dtype=jnp.int32)[None, :]
    select_low = selector.astype(jnp.bfloat16)
    adapter_selector_full = selector.astype(jnp.float32)
    down_rank_rows = lax.all_gather(
        adapter_down_weight.astype(jnp.bfloat16), "wide", axis=1, tiled=True
    )
    up_weight_portion = lax.all_gather(
        adapter_up_weight.astype(jnp.bfloat16), "narrow", axis=1, tiled=True
    )
    up_rank_rows = lax.all_gather(up_weight_portion, "wide", axis=0, tiled=True)
    spread = jnp.dot(tokens, down_rank_rows, preferred_element_type=jnp.float32)
    lowrank_codes = lax.psum(packed_adapter_index(spread, adapter_selector_full), "narrow")
    code_low = lowrank_codes.astype(jnp.bfloat16)
    wide_adapter_index = expand_codes(code_low, select_low)
    summed = lax.psum(
        jnp.dot(tokens, frozen_value_weight, preferred_element_type=jnp.float32), "narrow"
    )
    frozen_value_rows = lax.dynamic_slice_in_dim(summed, row_start, row_count, 0)
    wide_rows = lax.dynamic_slice_in_dim(wide_adapter_index, row_start, row_count, 0)
    rank_output_delta = jnp.dot(wide_rows, up_rank_rows, preferred_element_type=jnp.float32)
    values = (frozen_value_rows + adapter_scale * rank_output_delta).astype(jnp.bfloat16)
    grad_full = lax.all_gather(value_output_gradient, "narrow", axis=0, tiled=True)
    returned_spread_rows = jnp.einsum(
        "tc,kc->tk", grad_full, up_rank_rows, preferred_element_type=jnp.float32
    )
    returned_rank_rows = (
        adapter_scale * packed_adapter_index(returned_spread_rows, adapter_selector_full)
    ).astype(jnp.bfloat16)
    back_wide = expand_codes(returned_rank_rows, select_low)
    grad_tokens = (
        jnp.einsum("tc,dc->td", grad_full, frozen_value_weight, preferred_element_type=jnp.float32)
        + jnp.einsum("tk,dk->td", back_wide, down_rank_rows, preferred_element_type=jnp.float32)
    ).astype(jnp.bfloat16)
    rank_column_count = adapter_up_weight.shape[1]
    grad_columns = lax.dynamic_slice_in_dim(
        grad_full, narrow_index * rank_column_count, rank_column_count, 1
    )
    up_output_term = adapter_scale * jnp.einsum(
        "tk,tc->kc", wide_adapter_index, grad_columns, preferred_element_type=jnp.float32
    )
    up_weight_gradient = lax.psum_scatter(
        up_output_term.astype(jnp.bfloat16), "wide", scatter_dimension=0, tiled=True
    ).astype(jnp.float32)
    down_term = jnp.einsum("td,tk->dk", tokens, back_wide, preferred_element_type=jnp.float32)
    down_weight_gradient = lax.psum_scatter(
        down_term.astype(jnp.bfloat16), "wide", scatter_dimension=1, tiled=True
    ).astype(jnp.float32)
    learning_rate_columns = jnp.repeat(rates, ADAPTER_RANK)
    updated_down_weight, updated_down_moment_first, updated_down_moment_second = apply_adam_moments(
        adapter_down_weight,
        down_moment_first,
        down_moment_second,
        down_weight_gradient,
        learning_rate_columns[None, :],
    )
    updated_up_weight, updated_up_moment_first, updated_up_moment_second = apply_adam_moments(
        adapter_up_weight,
        up_moment_first,
        up_moment_second,
        up_weight_gradient,
        learning_rate_columns[:, None],
    )
    return (
        values,
        grad_tokens,
        updated_down_weight,
        updated_down_moment_first,
        updated_down_moment_second,
        updated_up_weight,
        updated_up_moment_first,
        updated_up_moment_second,
    )


def solution(mesh):
    return jax.shard_map(
        shards,
        mesh=mesh,
        in_specs=(
            P(("grid", "wide"), "narrow"),
            P("narrow", None),
            P(("grid", "wide"), None),
            P(("grid", "narrow"), "wide"),
            P(("grid", "wide"), "narrow"),
            P(("grid", "narrow"), "wide"),
            P(("grid", "narrow"), "wide"),
            P(("grid", "wide"), "narrow"),
            P(("grid", "wide"), "narrow"),
            P(("grid", "wide")),
            P(("grid", "wide", "narrow"), None),
        ),
        out_specs=(
            P(("grid", "wide", "narrow"), None),
            P(("grid", "wide"), "narrow"),
            P(("grid", "narrow"), "wide"),
            P(("grid", "narrow"), "wide"),
            P(("grid", "narrow"), "wide"),
            P(("grid", "wide"), "narrow"),
            P(("grid", "wide"), "narrow"),
            P(("grid", "wide"), "narrow"),
        ),
        check_vma=False,
    )
```

profile of v0, /device:TPU:0, one launch (start us, length us, event | category | flops | bytes accessed | tf_op | source)
XLA Modules:
  0.0 136.0 jit_solution(9642637931498109941)
XLA Ops:
  7.2 0.0 copy-start
  7.2 0.0 all-gather.2.cloned.1.call-start
  7.2 0.7 all-gather.2.cloned.1.call-update
  7.9 0.0 all-reduce.2.cloned.1.call-start
  8.0 0.8 copy-done
  8.8 5.8 %fusion.18 = f32[512,1024]{1,0:T(8,128)} fusion(bf16[512,2048]{1,0:T(8,128)(2,1)S(1)} %copy-done, bf16[2048,1024]{1,0:T(8,128)(2,1)} %param.12), kind=kOutput, calls=%fused_computation.30 | convolution fusion | flops 2147483648 | bytes 8388608 | tf_op jit(solution)/shard_map/dot_general | solution.py:70
  14.6 0.0 copy-start.4
  14.6 0.0 copy-start.1
  14.6 0.0 all-reduce.2.cloned.1.call-update
  14.6 0.0 reduce-scatter.5.cloned.1.call-start
  14.7 0.7 copy-done.4
  15.4 6.2 %all_gather.13 = bf16[32,1024]{1,0:T(8,128)(2,1)S(1)} all-gather(bf16[32,256]{1,0:T(8,128)(2,1)S(1)} %convert_element_type.55), channel_id=1, replica_groups=mesh['grid'=2,'wide'=4,'narrow'=4] {'narrow'}, dimensions={1}, use_global_device_ids=true | all-gather | bytes 81920 | tf_op jit(solution)/shard_map/all_gather | solution.py:61
  21.5 0.0 copy-start.5
  21.5 0.0 copy-start.6
  21.5 14.7 %all_gather.14 = bf16[128,1024]{1,0:T(8,128)(2,1)S(1)} all-gather(bf16[32,1024]{1,0:T(8,128)(2,1)S(1)} %all_gather.13), channel_id=1, replica_groups=mesh['grid'=2,'wide'=4,'narrow'=4] {'wide'}, dimensions={0}, use_global_device_ids=true | all-gather | bytes 327680 | tf_op jit(solution)/shard_map/all_gather | solution.py:64
  36.3 0.0 copy-done.1
  36.3 15.9 %all_gather.12 = bf16[2048,128]{0,1:T(8,128)(2,1)S(1)} all-gather(bf16[2048,32]{0,1:T(8,128)(2,1)S(1)} %convert_element_type.52), channel_id=1, replica_groups=mesh['grid'=2,'wide'=4,'narrow'=4] {'wide'}, dimensions={1}, use_global_device_ids=true | all-gather | bytes 655360 | tf_op jit(solution)/shard_map/all_gather | solution.py:58
  52.2 0.8 fusion.19
  53.0 0.0 copy-done.5
  53.0 0.0 copy-done.6
  53.0 0.1 broadcast_in_dim.2
  53.1 0.1 mul.161
  53.2 0.0 all-gather.2.cloned.1.call-done
  53.2 1.7 %fusion.21 = f32[512,128]{0,1:T(8,128)S(1)} fusion(bf16[512,1024]{1,0:T(8,128)(2,1)} %all-gather.2.cloned.1.call-done, bf16[128,1024]{1,0:T(8,128)(2,1)S(1)} %all_gather.14), kind=kOutput, calls=%fused_computation.33 | convolution fusion | flops 134217728 | bytes 1572864 | tf_op jit(solution)/shard_map/tc,kc->tk/dot_general | solution.py:77
  54.9 0.1 multiply_reduce_fusion
  55.0 10.3 %psum.15 = bf16[512,16]{0,1:T(8,128)(2,1)S(1)} all-reduce(f32[512,16]{0,1:T(8,128)S(1)} %get-tuple-element.9), channel_id=1, replica_groups=mesh['grid'=2,'wide'=4,'narrow'=4] {'narrow'}, use_global_device_ids=true, to_apply=%region_2.0 | all-reduce | flops 8192 | bytes 49152 | tf_op jit(solution)/shard_map/psum | solution.py:66
  65.3 1.8 %fusion.3 = bf16[128,256]{1,0:T(8,128)(2,1)} fusion(bf16[512,128]{0,1:T(8,128)(2,1)S(1)} %bitcast.25, bf16[512,1024]{1,0:T(8,128)(2,1)} %all-gather.2.cloned.1.call-done, s32[]{:T(128)S(6)} %select_n.8), kind=kOutput, calls=%fused_computation.7 | convolution fusion | flops 33619968 | bytes 458756 | tf_op jit(solution)/shard_map/tk,tc->kc/dot_general | solution.py:92
  67.1 0.0 reduce-scatter.5.cloned.1.call-update
  67.1 0.0 reduce-scatter.3.cloned.1.call-start
  67.2 1.2 fusion
  68.4 0.0 reduce-scatter.3.cloned.1.call-update
  68.5 15.1 %all-reduce.2.cloned.1.call-done = f32[512,1024]{1,0:T(8,128)} async-done(((f32[512,1024]{1,0:T(8,128)}), f32[512,1024]{1,0:T(8,128)}) %all-reduce.2.cloned.1.call-update) | async-done | bytes 2097168 | tf_op jit(solution)/shard_map/psum | solution.py:69
  83.5 2.0 %fusion.2 = bf16[128,1024]{1,0:T(8,128)(2,1)} fusion(bf16[128,1024]{1,0:T(8,128)(2,1)S(1)} %all_gather.14, f32[512,1024]{1,0:T(8,128)} %all-reduce.2.cloned.1.call-done, s32[]{:T(128)S(6)} %select_n.7, bf16[512,128]{0,1:T(8,128)(2,1)S(1)} %bitcast.26), kind=kOutput, calls=%fused_computation.5 | convolution fusion | flops 33947648 | bytes 1082368 | tf_op jit(solution)/shard_map/dot_general | solution.py:74
  85.5 4.9 %fusion.20 = f32[512,2048]{1,0:T(8,128)S(1)} fusion(bf16[512,1024]{1,0:T(8,128)(2,1)} %all-gather.2.cloned.1.call-done, bf16[2048,1024]{1,0:T(8,128)(2,1)} %param.12), kind=kOutput, calls=%fused_computation.32 | convolution fusion | flops 2147483648 | bytes 9437184 | tf_op jit(solution)/shard_map/tc,dc->td/dot_general | solution.py:85
  90.4 0.0 copy-start.2
  90.4 0.0 copy-start.3
  90.5 2.1 %add_convert_fusion = bf16[512,2048]{1,0:T(8,128)(2,1)} fusion(f32[512,2048]{1,0:T(8,128)S(1)} %fusion.20, bf16[512,128]{0,1:T(8,128)(2,1)S(1)} %bitcast.22, bf16[2048,128]{0,1:T(8,128)(2,1)S(1)} %all_gather.12), kind=kOutput, calls=%fused_computation | convolution fusion | flops 270532608 | bytes 6946816 | tf_op jit(solution)/shard_map/tk,dk->td/dot_general | solution.py:86
  92.5 13.1 %reduce-scatter.5.cloned.1.call-done = bf16[32,256]{1,0:T(8,128)(2,1)} async-done(((bf16[128,256]{1,0:T(8,128)(2,1)}), bf16[32,256]{1,0:T(8,128)(2,1)}) %reduce-scatter.5.cloned.1.call-update) | async-done | bytes 16400 | tf_op jit(solution)/shard_map/reduce_scatter | solution.py:95
  105.6 1.5 %divide_subtract_fusion.1 = (f32[32,256]{1,0:T(8,128)}, f32[32,256]{1,0:T(8,128)}, f32[32,256]{1,0:T(8,128)}) fusion(f32[32,256]{1,0:T(8,128)} %param.15, f32[32]{0:T(128)S(1)} %mul.161, bf16[32,256]{1,0:T(8,128)(2,1)} %reduce-scatter.5.cloned.1.call-done, f32[32,256]{1,0:T(8,128)} %param.18, f32[32,256]{1,0:T(8,128)} %param.19), kind=kLoop, calls=%fused_computation.22 | loop fusion | flops 106496 | bytes 213120 | tf_op jit(solution)/shard_map/sub | solution.py:32
  107.1 20.5 %reduce-scatter.3.cloned.1.call-done = bf16[2048,32]{0,1:T(8,128)(2,1)} async-done(((bf16[2048,128]{0,1:T(8,128)(2,1)}), bf16[2048,32]{0,1:T(8,128)(2,1)}) %reduce-scatter.3.cloned.1.call-update) | async-done | bytes 131088 | tf_op jit(solution)/shard_map/reduce_scatter | solution.py:99
  127.6 0.0 copy-done.2
  127.6 0.0 copy-done.3
  127.6 1.9 %divide_subtract_fusion = (f32[2048,32]{0,1:T(8,128)}, f32[2048,32]{0,1:T(8,128)}, f32[2048,32]{0,1:T(8,128)}) fusion(f32[2048,32]{0,1:T(8,128)S(1)} %copy-done.1, f32[32]{0:T(128)S(1)} %mul.161, bf16[2048,32]{0,1:T(8,128)(2,1)} %reduce-scatter.3.cloned.1.call-done, f32[2048,32]{0,1:T(8,128)S(1)} %copy-done.2, f32[2048,32]{0,1:T(8,128)S(1)} %copy-done.3), kind=kLoop, calls=%fused_computation.13 | loop fusion | flops 851968 | bytes 1704064 | tf_op jit(solution)/shard_map/sub | solution.py:32
  (5 shorter events, 0.1 us)
Async XLA Ops:
  7.2 1.6 %copy-start = (bf16[512,2048]{1,0:T(8,128)(2,1)S(1)}, bf16[512,2048]{1,0:T(8,128)(2,1)}, u32[]{:S(2)}) copy-start(bf16[512,2048]{1,0:T(8,128)(2,1)} %param.11) | copy-start | bytes 6291460
  7.2 46.0 %all-gather.2.cloned.1.call-start = ((), (), s32[]{:S(2)}) async-start(), calls=%async_computation.3 | async-start | bytes 1310720 | tf_op jit(solution)/shard_map/all_gather | solution.py:76
  7.9 75.6 %all-reduce.2.cloned.1.call-start = ((), (), s32[]{:S(2)}) async-start(), calls=%async_computation.2 | async-start | bytes 4194304 | tf_op jit(solution)/shard_map/psum | solution.py:69
  14.6 0.8 copy-start.4
  14.6 21.7 %copy-start.1 = (f32[2048,32]{0,1:T(8,128)S(1)}, f32[2048,32]{0,1:T(8,128)}, u32[]{:S(2)}) copy-start(f32[2048,32]{0,1:T(8,128)} %param.14) | copy-start | bytes 786436
  14.6 90.9 %reduce-scatter.5.cloned.1.call-start = ((), (), s32[]{:S(2)}) async-start(), calls=%async_computation.5 | async-start | bytes 81920 | tf_op jit(solution)/shard_map/reduce_scatter | solution.py:95
  21.5 31.5 %copy-start.5 = (s32[512,1]{0,1:T(1,128)S(1)}, s32[512,1]{0,1:T(1,128)}, u32[]{:S(2)}) copy-start(s32[512,1]{0,1:T(1,128)} %param.13) | copy-start | bytes 6148
  21.5 31.5 %copy-start.6 = (f32[2]{0:T(128)S(1)}, f32[2]{0:T(128)}, u32[]{:S(2)}) copy-start(f32[2]{0:T(128)} %param.20) | copy-start | bytes 28
  67.1 60.4 %reduce-scatter.3.cloned.1.call-start = ((), (), s32[]{:S(2)}) async-start(), calls=%async_computation.4 | async-start | bytes 655360 | tf_op jit(solution)/shard_map/reduce_scatter | solution.py:99
  90.4 37.1 %copy-start.2 = (f32[2048,32]{0,1:T(8,128)S(1)}, f32[2048,32]{0,1:T(8,128)}, u32[]{:S(2)}) copy-start(f32[2048,32]{0,1:T(8,128)} %param.16) | copy-start | bytes 786436
  90.4 37.1 %copy-start.3 = (f32[2048,32]{0,1:T(8,128)S(1)}, f32[2048,32]{0,1:T(8,128)}, u32[]{:S(2)}) copy-start(f32[2048,32]{0,1:T(8,128)} %param.17) | copy-start | bytes 786436
Sparse Core Ops, SparseCore 0:
  9.6 19.4 all-gather.1
  32.0 51.5 all-reduce.1
  86.5 19.0 reduce-scatter.4
  107.7 19.8 reduce-scatter.2
where the time goes:
time: 136 us
  waiting for transfers between devices  49.4 us (36%)
  blocking collectives  47 us (35%)
  matrix products  20.4 us (15%)
  between operations  13.9 us (10%)
  other arithmetic  3.49 us (3%)
  local copies, waits for them, and re-layouts  1.66 us (1%)
    reduce_scatter x1, waiting for transfers between devices, shards(): lax.psum_scatter(down_term.astype(jnp.bfloat16), 'wide', scatter_dimensio...  20.5 us
    all_gather x1, blocking collectives, shards(): lax.all_gather(adapter_down_weight.astype(jnp.bfloat16), 'wide', axis=1,...  15.9 us
    psum x1, waiting for transfers between devices, shards(): lax.psum(jnp.dot(tokens, frozen_value_weight, preferred_element_type=jnp....  15.1 us
    all_gather x1, blocking collectives, shards(): up_rank_rows = lax.all_gather(up_weight_portion, 'wide', axis=0, tiled=True)  14.7 us
    reduce_scatter x1, waiting for transfers between devices, shards(): lax.psum_scatter(up_output_term.astype(jnp.bfloat16), 'wide', scatter_dim...  13.1 us
    psum x1, blocking collectives, shards(): lax.psum(packed_adapter_index(spread, adapter_selector_full), 'narrow')  10.3 us
    all_gather x1, blocking collectives, shards(): lax.all_gather(adapter_up_weight.astype(jnp.bfloat16), 'narrow', axis=1,...  6.17 us
    dot_general x1, matrix products, shards(): jnp.dot(tokens, frozen_value_weight, preferred_element_type=jnp.float32)  5.84 us
  transfers between devices with their start and end apart: 4, of which 3 were waited for; matrix products, arithmetic and copies ran while one was open for 16% of the time, Pallas kernels for 0%

commit v1 on v0

--- a/solution.py
+++ b/solution.py
@@ -1,6 +1,10 @@
+import functools
+
 import jax
 import jax.numpy as jnp
 from jax import lax
+from jax.experimental import pallas as pl
+from jax.experimental.pallas import tpu as pltpu
 from jax.sharding import PartitionSpec as P
 
 ADAPTER_RANK = 16
@@ -126,9 +130,442 @@
     )
 
 
+MESH = pl.DeviceIdType.MESH
+HALVES = 2
+
+
+def dot_nn(a, b):
+    return lax.dot_general(a, b, (((1,), (0,)), ((), ())), preferred_element_type=jnp.float32)
+
+
+def dot_nt(a, b):
+    return lax.dot_general(a, b, (((1,), (1,)), ((), ())), preferred_element_type=jnp.float32)
+
+
+def fused_kernel(
+    wide,
+    tok_hbm, w_hbm, idx_hbm, down_hbm, up_hbm, dm1_hbm, dm2_hbm, um1_hbm, um2_hbm, rates_ref, g_hbm,
+    val_out, gt_out, dw_out, dm1_out, dm2_out, uw_out, um1_out, um2_out,
+    tok, w, idx, g, upf, downf, dw, dm1, dm2, uw, um1, um2,
+    psend, precv, pacc, xsend, xrecv, bsend, brecv, bnat, csend, crecv, cnat,
+    dpart, rs_stage, rs_left, rs_right, gt_acc, gt, gu_stage, gu_recv, vals,
+    load_sem, store_sem, send_sem, recv_sem,
+):
+    z = lax.axis_index("wide")
+    me = lax.axis_index("narrow")
+    x, c = me // 2, me % 2
+    xo, co = 1 - x, 1 - c
+    block = {0: me, 1: x * 2 + co, 2: xo * 2 + c, 3: xo * 2 + co}
+    place = {3: 0, 1: 1, 2: 2, 0: 3}
+    order = (3, 1, 2, 0)
+    T, D = tok.shape
+    C = w.shape[1]
+    R, CC = T // 4, C // 4
+    K = dw.shape[0]
+    A = K * wide
+    members = A // ADAPTER_RANK
+    HD = D // HALVES
+
+    names = {}
+
+    def number(name):
+        return names.setdefault(name, len(names))
+
+    def remote(name, src_ref, dst_ref, device):
+        k = number(name)
+        return pltpu.make_async_remote_copy(
+            src_ref=src_ref, dst_ref=dst_ref, send_sem=send_sem.at[k], recv_sem=recv_sem.at[k],
+            device_id=device, device_id_type=MESH,
+        )
+
+    sent = []
+
+    def send(name, src_ref, dst_ref, device):
+        copy = remote(name, src_ref, dst_ref, device)
+        copy.start()
+        sent.append(copy)
+
+    def arrived(name, ref):
+        remote(name, ref, ref, {"narrow": block[1]}).wait_recv()
+
+    loads = {}
+
+    def load(name, src_ref, dst_ref):
+        copy = pltpu.make_async_copy(src_ref, dst_ref, load_sem.at[len(loads)])
+        loads[name] = copy
+        copy.start()
+
+    stores = []
+
+    def store(src_ref, dst_ref):
+        copy = pltpu.make_async_copy(src_ref, dst_ref, store_sem.at[len(stores)])
+        stores.append(copy)
+        copy.start()
+
+    def rows(m):
+        return pl.ds(place[m] * R, R)
+
+    def natural(j):
+        return pl.ds(pl.multiple_of(j * R, R), R)
+
+    def column(j):
+        return pl.ds(pl.multiple_of(j * CC, CC), CC)
+
+    def shard(j):
+        return pl.ds(pl.multiple_of(j * K, K), K)
+
+    def half(h):
+        return pl.ds(h * HD, HD)
+
+    load("up", up_hbm, uw)
+    load("down", down_hbm, dw)
+    load("g", g_hbm, g.at[rows(0)])
+    for m in (3, 1):
+        load(("tok", m), tok_hbm.at[natural(block[m])], tok.at[rows(m)])
+    for q in range(4):
+        load(("w", q), w_hbm.at[:, pl.ds(q * CC, CC)], w.at[:, pl.ds(q * CC, CC)])
+    for m in (2, 0):
+        load(("tok", m), tok_hbm.at[natural(block[m])], tok.at[rows(m)])
+    for m in order:
+        load(("idx", m), idx_hbm.at[:, natural(block[m])], idx.at[:, rows(m)])
+    for name, src_ref, dst_ref in (
+        ("dm1", dm1_hbm, dm1), ("dm2", dm2_hbm, dm2), ("um1", um1_hbm, um1), ("um2", um2_hbm, um2)
+    ):
+        load(name, src_ref, dst_ref)
+
+    barrier = pltpu.get_barrier_semaphore()
+    for m in (1, 2, 3):
+        pl.semaphore_signal(barrier, inc=1, device_id={"narrow": block[m]}, device_id_type=MESH)
+    for d in range(1, wide):
+        pl.semaphore_signal(
+            barrier, inc=1, device_id={"wide": lax.rem(z + d, wide)}, device_id_type=MESH
+        )
+    loads["up"].wait()
+    upf[shard(z), column(me)] = uw[...].astype(jnp.bfloat16)
+    loads["down"].wait()
+    downf[shard(z), :] = dw[...].astype(jnp.bfloat16)
+    loads["g"].wait()
+    pl.semaphore_wait(barrier, 3 + wide - 1)
+
+    for d in range(1, wide):
+        mine = upf.at[shard(z), column(me)]
+        send(("up", d), mine, mine, {"wide": lax.rem(z + d, wide)})
+
+    chain_sent = []
+
+    def guarded_send(cond, name, src_ref, dst_ref, device):
+        copy = remote(name, src_ref, dst_ref, device)
+        pl.when(cond)(copy.start)
+        chain_sent.append((cond, copy))
+
+    def down_step(s):
+        for h in range(HALVES):
+            if s >= 1:
+                @pl.when(z - s >= 0)
+                def _():
+                    arrived(("down_r", s - 1, h), downf.at[shard(z - s), half(h)])
+
+            if s <= wide - 2:
+                part = downf.at[shard(jnp.maximum(z - s, 0)), half(h)]
+                guarded_send(
+                    (z - s >= 0) & (z < wide - 1), ("down_r", s, h), part, part,
+                    {"wide": jnp.minimum(z + 1, wide - 1)},
+                )
+            if s >= 1:
+                @pl.when(z + s <= wide - 1)
+                def _():
+                    arrived(("down_l", s - 1, h), downf.at[shard(z + s), half(h)])
+
+            if s <= wide - 2:
+                part = downf.at[shard(jnp.minimum(z + s, wide - 1)), half(h)]
+                guarded_send(
+                    (z + s <= wide - 1) & (z > 0), ("down_l", s, h), part, part,
+                    {"wide": jnp.maximum(z - 1, 0)},
+                )
+
+    down_step(0)
+
+    for m, core in ((2, c), (3, co)):
+        part = column(xo * 2 + core)
+        send(("g", m, 0), g.at[rows(0), part], g.at[rows(m), part], {"narrow": block[m]})
+    send("g_sib", g.at[rows(0)], g.at[rows(1)], {"narrow": block[1]})
+    for m, core in ((2, c), (3, co)):
+        part = column(x * 2 + core)
+        send(("g", m, 1), g.at[rows(0), part], g.at[rows(m), part], {"narrow": block[m]})
+
+    loads["tok", 3].wait()
+    loads["tok", 1].wait()
+    for q in range(4):
+        loads["w", q].wait()
+        cols = pl.ds(q * CC, CC)
+        psend[:, cols] = dot_nn(tok[0 : 2 * R, :], w[:, cols]).astype(jnp.bfloat16)
+    send("p", psend, precv, {"narrow": block[1]})
+
+    for m in order:
+        loads["idx", m].wait()
+    adapter = lax.broadcasted_iota(jnp.int32, (A, T), 0) // ADAPTER_RANK
+
+    def member():
+        return adapter == jnp.broadcast_to(idx[...], (A, T))
+
+    def pack(full):
+        chosen = jnp.where(member(), full, 0.0)
+        total = chosen[0:ADAPTER_RANK]
+        for a in range(1, members):
+            total = total + chosen[a * ADAPTER_RANK : (a + 1) * ADAPTER_RANK]
+        return total
+
+    def spread_out(packed):
+        return jnp.where(member(), jnp.concatenate([packed] * members, axis=0), 0.0)
+
+    def exchange(name, packed, out, box):
+        low = packed.astype(jnp.bfloat16)
+        for m in order:
+            out[:, natural(block[m])] = low[:, place[m] * R : (place[m] + 1) * R]
+        for m in (2, 3, 1):
+            send((name, m), out, box.at[m - 1], {"narrow": block[m]})
+
+    def total_of(name, packed, box, nat):
+        for m in (1, 2, 3):
+            arrived((name, m), box.at[m - 1])
+        nat[...] = box[0].astype(jnp.float32) + box[1].astype(jnp.float32) + box[2].astype(jnp.float32)
+        return packed + jnp.concatenate([nat[:, natural(block[m])] for m in order], axis=1)
+
+    for d in range(1, wide):
+        arrived(("up", d), upf.at[shard(lax.rem(z - d + wide, wide)), column(me)])
+    arrived("g_sib", g.at[rows(1)])
+    for m in (2, 3):
+        arrived(("g", m, 0), g.at[rows(m), column(me)])
+    back_part = pack(dot_nt(upf[:, column(me)], g[:, column(me)]))
+    exchange("back", back_part, bsend, brecv)
+    for m, to in ((2, 3), (3, 2)):
+        send(("g_fwd", m, 0), g.at[rows(m), column(me)], g.at[rows(to), column(me)], {"narrow": block[1]})
+    for m in (2, 1):
+        mine = upf.at[:, column(me)]
+        send(("up_x", m), mine, mine, {"narrow": block[m]})
+
+    down_step(1)
+
+    loads["tok", 2].wait()
+    loads["tok", 0].wait()
+    for q in range(4):
+        cols = pl.ds(q * CC, CC)
+        pacc[:, cols] = dot_nn(tok[2 * R :, :], w[:, cols])
+    arrived("p", precv)
+    xsend[...] = (pacc[0:R] + precv[0:R].astype(jnp.float32)).astype(jnp.bfloat16)
+    send("px", xsend, xrecv, {"narrow": block[2]})
+
+    back = 2.0 * total_of("back", back_part, brecv, bnat)
+    back_wide_t = spread_out(back)
+    back_low = back_wide_t.astype(jnp.bfloat16)
+    for h in range(HALVES):
+        dpart[:, half(h)] = dot_nn(back_low, tok[:, half(h)])
+
+    rs_sent = []
+
+    def rs_step(k):
+        for right in (True, False):
+            j = wide - 1 - k if right else k
+            box = rs_left if right else rs_right
+            name = "rs_r" if right else "rs_l"
+            ahead = (j > z) if right else (j < z)
+            follows = (z > 0) if right else (z < wide - 1)
+            target = jnp.minimum(z + 1, wide - 1) if right else jnp.maximum(z - 1, 0)
+            for h in range(HALVES):
+                own = dpart.at[pl.ds(j * K, K), half(h)]
+                stage = rs_stage.at[j, :, half(h)]
+                landing = box.at[j, :, half(h)]
+
+                @pl.when(ahead & follows)
+                def _():
+                    arrived((name, k, h), landing)
+                    stage[...] = (own[...] + landing[...].astype(jnp.float32)).astype(jnp.bfloat16)
+
+                @pl.when(ahead & jnp.logical_not(follows))
+                def _():
+                    stage[...] = own[...].astype(jnp.bfloat16)
+
+                copy = remote((name, k, h), stage, landing, {"wide": target})
+                pl.when(ahead)(copy.start)
+                rs_sent.append((ahead, copy))
+
+    rs_step(0)
+    for s in range(2, wide):
+        down_step(s)
+
+    for m, to in ((2, 3), (3, 2)):
+        part = column(xo * 2 + c)
+        arrived(("g", m, 1), g.at[rows(m), part])
+        send(("g_fwd", m, 1), g.at[rows(m), part], g.at[rows(to), part], {"narrow": block[1]})
+    arrived(("up_x", 2), upf.at[:, column(block[2])])
+    part = upf.at[:, column(block[2])]
+    send("up_fwd", part, part, {"narrow": block[1]})
+
+    code_part = pack(dot_nt(tok[...], downf[...]).T)
+    exchange("code", code_part, csend, crecv)
+
+    for m in (2, 3):
+        arrived(("g_fwd", 5 - m, 0), g.at[rows(m), column(block[1])])
+        arrived(("g_fwd", 5 - m, 1), g.at[rows(m), column(block[3])])
+    back_rows = back_wide_t.T.astype(jnp.bfloat16)
+
+    def grad_tokens(part, parts):
+        width = D // parts
+        span = pl.ds(part * width, width)
+        gt[:, span] = (dot_nt(g[...], w[span, :]) + dot_nn(back_rows, downf[:, span])).astype(jnp.bfloat16)
+        for m in order:
+            store(gt.at[rows(m), span], gt_out.at[natural(block[m]), span])
+
+    grad_tokens(0, 4)
+    if wide > 2:
+        rs_step(1)
+
+    code = total_of("code", code_part, crecv, cnat)
+    code_wide_t = spread_out(code)
+    code_low = code_wide_t.astype(jnp.bfloat16)
+    gu_stage[...] = (2.0 * dot_nn(code_low, g[:, column(me)])).astype(jnp.bfloat16)
+    for d in range(1, wide):
+        to = lax.rem(z + d, wide)
+        send(("gu", d), gu_stage.at[shard(to)], gu_recv.at[d], {"wide": to})
+
+    grad_tokens(1, 4)
+    for k in range(2, wide - 1):
+        rs_step(k)
+    grad_tokens(2, 4)
+    grad_tokens(3, 4)
+
+    arrived(("up_x", 1), upf.at[:, column(block[1])])
+    arrived("up_fwd", upf.at[:, column(block[3])])
+    code_rows = code_wide_t[:, place[0] * R : (place[0] + 1) * R].T.astype(jnp.bfloat16)
+    delta = dot_nn(code_rows, upf[...])
+    arrived("px", xrecv)
+    vals[...] = (
+        pacc[R : 2 * R] + precv[R : 2 * R].astype(jnp.float32) + xrecv[...].astype(jnp.float32) + 2.0 * delta
+    ).astype(jnp.bfloat16)
+    store(vals, val_out)
+
+    owner = lax.broadcasted_iota(jnp.int32, (K, 1), 0) // ADAPTER_RANK
+    rate = jnp.zeros((K, 1), jnp.float32)
+    for a in range(K // ADAPTER_RANK):
+        rate = jnp.where(owner == a, rates_ref[a], rate)
+
+    grad_up = gu_stage[shard(z), :].astype(jnp.float32)
+    for d in range(1, wide):
+        arrived(("gu", d), gu_recv.at[d])
+        grad_up = grad_up + gu_recv[d].astype(jnp.float32)
+    loads["um1"].wait()
+    loads["um2"].wait()
+    uw[...], um1[...], um2[...] = apply_adam_moments(uw[...], um1[...], um2[...], grad_up, rate)
+    store(uw, uw_out)
+    store(um1, um1_out)
+    store(um2, um2_out)
+
+    loads["dm1"].wait()
+    loads["dm2"].wait()
+    for h in range(HALVES):
+        cols = half(h)
+        for j in range(wide):
+            if j > 0:
+                @pl.when(z == j)
+                def _():
+                    landing = rs_left.at[j, :, cols]
+                    arrived(("rs_r", wide - 1 - j, h), landing)
+                    own = dpart.at[pl.ds(j * K, K), cols]
+                    own[...] = own[...] + landing[...].astype(jnp.float32)
+
+            if j < wide - 1:
+                @pl.when(z == j)
+                def _():
+                    landing = rs_right.at[j, :, cols]
+                    arrived(("rs_l", j, h), landing)
+                    own = dpart.at[pl.ds(j * K, K), cols]
+                    own[...] = own[...] + landing[...].astype(jnp.float32)
+
+        grad_down = dpart[shard(z), cols]
+        dw[:, cols], dm1[:, cols], dm2[:, cols] = apply_adam_moments(
+            dw[:, cols], dm1[:, cols], dm2[:, cols], grad_down, rate
+        )
+        store(dw.at[:, cols], dw_out.at[:, cols])
+        store(dm1.at[:, cols], dm1_out.at[:, cols])
+        store(dm2.at[:, cols], dm2_out.at[:, cols])
+
+    for copy in sent:
+        copy.wait_send()
+    for cond, copy in chain_sent + rs_sent:
+        pl.when(cond)(copy.wait_send)
+    for copy in stores:
+        copy.wait()
+
+
+def fused_shards(
+    tokens,
+    frozen_value_weight,
+    token_adapter_index,
+    adapter_down_weight,
+    adapter_up_weight,
+    down_moment_first,
+    down_moment_second,
+    up_moment_first,
+    up_moment_second,
+    rates,
+    value_output_gradient,
+):
+    wide = lax.axis_size("wide")
+    T, D = tokens.shape
+    C = frozen_value_weight.shape[1]
+    R, CC = T // 4, C // 4
+    K = adapter_down_weight.shape[1]
+    A = K * wide
+    f32, low = jnp.float32, jnp.bfloat16
+    shape = jax.ShapeDtypeStruct
+    remotes = 2 * (wide - 1) + 16 + 4 * HALVES * (wide - 1) + 8
+    any_spec = pl.BlockSpec(memory_space=pl.ANY)
+    outs = pl.pallas_call(
+        functools.partial(fused_kernel, wide),
+        out_shape=(
+            shape((R, C), low), shape((T, D), low),
+            shape((K, D), f32), shape((K, D), f32), shape((K, D), f32),
+            shape((K, CC), f32), shape((K, CC), f32), shape((K, CC), f32),
+        ),
+        in_specs=[any_spec] * 9 + [pl.BlockSpec(memory_space=pltpu.SMEM), any_spec],
+        out_specs=(any_spec,) * 8,
+        scratch_shapes=[
+            pltpu.VMEM((T, D), low), pltpu.VMEM((D, C), low), pltpu.VMEM((1, T), jnp.int32),
+            pltpu.VMEM((T, C), low), pltpu.VMEM((A, C), low), pltpu.VMEM((A, D), low),
+            pltpu.VMEM((K, D), f32), pltpu.VMEM((K, D), f32), pltpu.VMEM((K, D), f32),
+            pltpu.VMEM((K, CC), f32), pltpu.VMEM((K, CC), f32), pltpu.VMEM((K, CC), f32),
+            pltpu.VMEM((2 * R, C), low), pltpu.VMEM((2 * R, C), low), pltpu.VMEM((2 * R, C), f32),
+            pltpu.VMEM((R, C), low), pltpu.VMEM((R, C), low),
+            pltpu.VMEM((ADAPTER_RANK, T), low), pltpu.VMEM((3, ADAPTER_RANK, T), low),
+            pltpu.VMEM((ADAPTER_RANK, T), f32),
+            pltpu.VMEM((ADAPTER_RANK, T), low), pltpu.VMEM((3, ADAPTER_RANK, T), low),
+            pltpu.VMEM((ADAPTER_RANK, T), f32),
+            pltpu.VMEM((A, D), f32), pltpu.VMEM((wide, K, D), low),
+            pltpu.VMEM((wide, K, D), low), pltpu.VMEM((wide, K, D), low),
+            pltpu.VMEM((8, 128), f32), pltpu.VMEM((T, D), low),
+            pltpu.VMEM((A, CC), low), pltpu.VMEM((wide, K, CC), low), pltpu.VMEM((R, C), low),
+            pltpu.SemaphoreType.DMA((20,)), pltpu.SemaphoreType.DMA((16 + 4 + 3 * HALVES,)),
+            pltpu.SemaphoreType.DMA((remotes,)), pltpu.SemaphoreType.DMA((remotes,)),
+        ],
+        compiler_params=pltpu.CompilerParams(
+            collective_id=0, has_side_effects=True, vmem_limit_bytes=50 * 1024 * 1024
+        ),
+        cost_estimate=pl.CostEstimate(
+            flops=2 * (2 * T * D * C + 3 * T * D * A), bytes_accessed=12 * 1024 * 1024, transcendentals=0
+        ),
+    )(
+        tokens, frozen_value_weight, token_adapter_index.reshape(1, T),
+        adapter_down_weight.T, adapter_up_weight,
+        down_moment_first.T, down_moment_second.T, up_moment_first, up_moment_second,
+        rates, value_output_gradient,
+    )
+    values, grad_tokens, dw, dm1, dm2, uw, um1, um2 = outs
+    return (values, grad_tokens, dw.T, dm1.T, dm2.T, uw, um1, um2)
+
+
 def solution(mesh):
     return jax.shard_map(
-        shards,
+        fused_shards if mesh.shape["narrow"] == 4 and mesh.shape["wide"] > 1 else shards,
         mesh=mesh,
         in_specs=(
             P(("grid", "wide"), "narrow"),

time: 136 us -> 60.6 us (0.45)
  waiting for transfers between devices: 49.4 us -> 0 us
  blocking collectives: 47 us -> 0 us
  Pallas kernels: 0 us -> 44.2 us
  matrix products: 20.4 us -> 0 us
  local copies, waits for them, and re-layouts: 1.66 us -> 15.2 us
  between operations: 13.9 us -> 0.67 us
  other arithmetic: 3.49 us -> 0 us
    pallas_call x0 -> x1, Pallas kernels: none -> 44.2 us  [fused_shards(): pl.pallas_call(functools.partial(fused_kernel, wide), out_shape=(shape((R...]
    all_gather x3 -> x0, blocking collectives: 36.8 us -> none  [the longest x1 15.9 us: shards(): lax.all_gather(adapter_down_weight.astype(jnp.bfloat16), 'wide', axis=1,...]
    reduce_scatter x2 -> x0, waiting for transfers between devices: 33.6 us -> none  [the longest x1 20.5 us: shards(): lax.psum_scatter(down_term.astype(jnp.bfloat16), 'wide', scatter_dimensio...]
    dot_general x8 -> x0, matrix products: 20.4 us -> none  [the longest x1 5.84 us: shards(): jnp.dot(tokens, frozen_value_weight, preferred_element_type=jnp.float32)]
    psum x1 -> x0, waiting for transfers between devices: 15.1 us -> none  [shards(): lax.psum(jnp.dot(tokens, frozen_value_weight, preferred_element_type=jnp....]
    unnamed x14 -> x26, local copies, waits for them, and re-layouts: 1.51 us -> 15.2 us
    psum x1 -> x0, blocking collectives: 10.3 us -> none  [shards(): lax.psum(packed_adapter_index(spread, adapter_selector_full), 'narrow')]
    sub x2 -> x0, other arithmetic: 3.38 us -> none  [apply_adam_moments(): return (parameter - update, first_new, second_new)]
  transfers between devices with their start and end apart: 4 -> 0, of which waited for: 3 -> 0; matrix products, arithmetic and copies ran while one was open for 16% -> 0% of each run, Pallas kernels for 0% -> 0%
where the time goes in v1:
time: 60.6 us; the launch traced here: 60.1 us
  Pallas kernels  44.2 us (73%)
  local copies, waits for them, and re-layouts  15.2 us (25%)
  between operations  0.67 us (1%)
    pallas_call x1, Pallas kernels, fused_shards(): pl.pallas_call(functools.partial(fused_kernel, wide), out_shape=(shape((R...  44.2 us
    unnamed x26, local copies, waits for them, and re-layouts  15.2 us

profile of v1, /device:TPU:0, one launch (start us, length us, event | category | flops | bytes accessed | tf_op | source)
XLA Modules:
  0.0 60.1 jit_solution(5259842484950603496)
XLA Ops:
  0.6 0.0 copy-start
  0.6 0.9 %copy-done = f32[2048,32]{0,1:T(8,128)S(1)} copy-done((f32[2048,32]{0,1:T(8,128)S(1)}, f32[2048,32]{0,1:T(8,128)}, u32[]{:S(2)}) %copy-start) | copy-done | bytes 262168
  1.6 0.0 copy-start.1
  1.6 0.9 %copy-done.1 = f32[2048,32]{0,1:T(8,128)S(1)} copy-done((f32[2048,32]{0,1:T(8,128)S(1)}, f32[2048,32]{0,1:T(8,128)}, u32[]{:S(2)}) %copy-start.1) | copy-done | bytes 262168
  2.5 0.0 copy-start.2
  2.5 0.9 %copy-done.2 = f32[2048,32]{0,1:T(8,128)S(1)} copy-done((f32[2048,32]{0,1:T(8,128)S(1)}, f32[2048,32]{0,1:T(8,128)}, u32[]{:S(2)}) %copy-start.2) | copy-done | bytes 262168
  3.5 0.0 copy-start.3
  3.5 0.9 %copy-done.3 = bf16[128,1024]{1,0:T(8,128)(2,1)S(1)} copy-done((bf16[128,1024]{1,0:T(8,128)(2,1)S(1)}, bf16[128,1024]{1,0:T(8,128)(2,1)}, u32[]{:S(2)}) %copy-start.3) | copy-done | bytes 262168
  4.4 0.0 copy-start.4
  4.4 0.8 %copy-done.4 = f32[32,256]{1,0:T(8,128)S(1)} copy-done((f32[32,256]{1,0:T(8,128)S(1)}, f32[32,256]{1,0:T(8,128)}, u32[]{:S(2)}) %copy-start.4) | copy-done | bytes 32792
  5.2 0.0 copy-start.5
  5.2 0.8 %copy-done.5 = f32[32,256]{1,0:T(8,128)S(1)} copy-done((f32[32,256]{1,0:T(8,128)S(1)}, f32[32,256]{1,0:T(8,128)}, u32[]{:S(2)}) %copy-start.5) | copy-done | bytes 32792
  6.0 0.0 copy-start.6
  6.0 0.8 %copy-done.6 = f32[32,256]{1,0:T(8,128)S(1)} copy-done((f32[32,256]{1,0:T(8,128)S(1)}, f32[32,256]{1,0:T(8,128)}, u32[]{:S(2)}) %copy-start.6) | copy-done | bytes 32792
  6.7 0.0 copy-start.7
  6.7 0.7 %copy-done.7 = s32[512,1]{0,1:T(1,128)S(1)} copy-done((s32[512,1]{0,1:T(1,128)S(1)}, s32[512,1]{0,1:T(1,128)}, u32[]{:S(2)}) %copy-start.7) | copy-done | bytes 2072
  7.4 0.0 copy-start.8
  7.4 0.7 %copy-done.8 = f32[2]{0:T(128)S(1)} copy-done((f32[2]{0:T(128)S(1)}, f32[2]{0:T(128)}, u32[]{:S(2)}) %copy-start.8) | copy-done | bytes 32
  8.1 44.2 %shard_map.170 = (bf16[128,1024]{1,0:T(8,128)(2,1)S(1)}, bf16[512,2048]{1,0:T(8,128)(2,1)}, f32[32,2048]{1,0:T(8,128)S(1)}, f32[32,2048]{1,0:T(8,128)S(1)}, f32[...) custom-call(bf16[512,2048]{1,0:T(8,128)(2,1)} %tok_hbm.1, ...), custom_call_target="tpu_custom_call" | custom-call | flops 5100273664 | bytes 12582912 | tf_op jit(solution)/shard_map/pallas_call | solution.py:523
  52.2 0.7 %copy.27 = bf16[128,1024]{1,0:T(8,128)(2,1)} copy(bf16[128,1024]{1,0:T(8,128)(2,1)S(1)} %get-tuple-element.32) | data formatting | bytes 524288
  52.9 3.2 %copy.28 = bf16[512,2048]{1,0:T(8,128)(2,1)} copy(bf16[512,2048]{1,0:T(8,128)(2,1)} %get-tuple-element.33) | data formatting | bytes 4194304
  56.1 0.7 %copy.29 = f32[2048,32]{0,1:T(8,128)} copy(f32[2048,32]{0,1:T(8,128)S(1)} %bitcast.9) | data formatting | bytes 524288
  56.8 0.7 %copy.30 = f32[2048,32]{0,1:T(8,128)} copy(f32[2048,32]{0,1:T(8,128)S(1)} %bitcast.8) | data formatting | bytes 524288
  57.5 0.7 %copy.31 = f32[2048,32]{0,1:T(8,128)} copy(f32[2048,32]{0,1:T(8,128)S(1)} %bitcast.7) | data formatting | bytes 524288
  58.2 0.6 %copy.32 = f32[32,256]{1,0:T(8,128)} copy(f32[32,256]{1,0:T(8,128)S(1)} %get-tuple-element.37) | data formatting | bytes 65536
  58.8 0.6 %copy.33 = f32[32,256]{1,0:T(8,128)} copy(f32[32,256]{1,0:T(8,128)S(1)} %get-tuple-element.38) | data formatting | bytes 65536
  59.4 0.6 %copy.34 = f32[32,256]{1,0:T(8,128)} copy(f32[32,256]{1,0:T(8,128)S(1)} %get-tuple-element.39) | data formatting | bytes 65536
Async XLA Ops:
  0.6 1.0 %copy-start = (f32[2048,32]{0,1:T(8,128)S(1)}, f32[2048,32]{0,1:T(8,128)}, u32[]{:S(2)}) copy-start(f32[2048,32]{0,1:T(8,128)} %param.14) | copy-start | bytes 786436
  1.6 0.9 %copy-start.1 = (f32[2048,32]{0,1:T(8,128)S(1)}, f32[2048,32]{0,1:T(8,128)}, u32[]{:S(2)}) copy-start(f32[2048,32]{0,1:T(8,128)} %param.16) | copy-start | bytes 786436
  2.5 0.9 %copy-start.2 = (f32[2048,32]{0,1:T(8,128)S(1)}, f32[2048,32]{0,1:T(8,128)}, u32[]{:S(2)}) copy-start(f32[2048,32]{0,1:T(8,128)} %param.17) | copy-start | bytes 786436
  3.5 0.9 %copy-start.3 = (bf16[128,1024]{1,0:T(8,128)(2,1)S(1)}, bf16[128,1024]{1,0:T(8,128)(2,1)}, u32[]{:S(2)}) copy-start(bf16[128,1024]{1,0:T(8,128)(2,1)} %g_hbm.1) | copy-start | bytes 786436
  4.4 0.8 %copy-start.4 = (f32[32,256]{1,0:T(8,128)S(1)}, f32[32,256]{1,0:T(8,128)}, u32[]{:S(2)}) copy-start(f32[32,256]{1,0:T(8,128)} %up_hbm.1) | copy-start | bytes 98308
  5.2 0.8 %copy-start.5 = (f32[32,256]{1,0:T(8,128)S(1)}, f32[32,256]{1,0:T(8,128)}, u32[]{:S(2)}) copy-start(f32[32,256]{1,0:T(8,128)} %um1_hbm.1) | copy-start | bytes 98308
  6.0 0.8 %copy-start.6 = (f32[32,256]{1,0:T(8,128)S(1)}, f32[32,256]{1,0:T(8,128)}, u32[]{:S(2)}) copy-start(f32[32,256]{1,0:T(8,128)} %um2_hbm.1) | copy-start | bytes 98308
  6.7 0.7 %copy-start.7 = (s32[512,1]{0,1:T(1,128)S(1)}, s32[512,1]{0,1:T(1,128)}, u32[]{:S(2)}) copy-start(s32[512,1]{0,1:T(1,128)} %param.13) | copy-start | bytes 6148
  7.4 0.7 %copy-start.8 = (f32[2]{0:T(128)S(1)}, f32[2]{0:T(128)}, u32[]{:S(2)}) copy-start(f32[2]{0:T(128)} %rates_ref.1) | copy-start | bytes 28

commit v2 on v1

--- a/solution.py
+++ b/solution.py
@@ -144,11 +144,11 @@
 
 def fused_kernel(
     wide,
-    tok_hbm, w_hbm, idx_hbm, down_hbm, up_hbm, dm1_hbm, dm2_hbm, um1_hbm, um2_hbm, rates_ref, g_hbm,
+    tok_hbm, w_hbm, idx_hbm, down_hbm, up_hbm, dm1_hbm, dm2_hbm, um1_hbm, um2_hbm, rates_hbm, g_hbm,
     val_out, gt_out, dw_out, dm1_out, dm2_out, uw_out, um1_out, um2_out,
     tok, w, idx, g, upf, downf, dw, dm1, dm2, uw, um1, um2,
     psend, precv, pacc, xsend, xrecv, bsend, brecv, bnat, csend, crecv, cnat,
-    dpart, rs_stage, rs_left, rs_right, gt_acc, gt, gu_stage, gu_recv, vals,
+    dpart, rs_stage, rs_left, rs_right, gt_acc, gt, gu_stage, gu_recv, vals, rates_ref,
     load_sem, store_sem, send_sem, recv_sem,
 ):
     z = lax.axis_index("wide")
@@ -229,7 +229,8 @@
     for m in order:
         load(("idx", m), idx_hbm.at[:, natural(block[m])], idx.at[:, rows(m)])
     for name, src_ref, dst_ref in (
-        ("dm1", dm1_hbm, dm1), ("dm2", dm2_hbm, dm2), ("um1", um1_hbm, um1), ("um2", um2_hbm, um2)
+        ("dm1", dm1_hbm, dm1), ("dm2", dm2_hbm, dm2), ("um1", um1_hbm, um1), ("um2", um2_hbm, um2),
+        ("rates", rates_hbm, rates_ref),
     ):
         load(name, src_ref, dst_ref)
 
@@ -444,6 +445,7 @@
     ).astype(jnp.bfloat16)
     store(vals, val_out)
 
+    loads["rates"].wait()
     owner = lax.broadcasted_iota(jnp.int32, (K, 1), 0) // ADAPTER_RANK
     rate = jnp.zeros((K, 1), jnp.float32)
     for a in range(K // ADAPTER_RANK):
@@ -495,6 +497,28 @@
         pl.when(cond)(copy.wait_send)
     for copy in stores:
         copy.wait()
+
+
+def write_kernel(*refs):
+    held, load_sem, store_sem = refs[16:24], refs[24], refs[25]
+    parts = 4
+    pieces = []
+    for k in (1, 0, 2, 3, 4, 5, 6, 7):
+        cuts = parts if k == 1 else 1
+        size = refs[k].shape[0] // cuts
+        for part in range(cuts):
+            rows, n = pl.ds(part * size, size), len(pieces)
+            pieces.append((
+                pltpu.make_async_copy(refs[k].at[rows], held[k].at[rows], load_sem.at[n]),
+                pltpu.make_async_copy(held[k].at[rows], refs[8 + k].at[rows], store_sem.at[n]),
+            ))
+    for load, _ in pieces:
+        load.start()
+    for load, store in pieces:
+        load.wait()
+        store.start()
+    for _, store in pieces:
+        store.wait()
 
 
 def fused_shards(
@@ -520,6 +544,7 @@
     shape = jax.ShapeDtypeStruct
     remotes = 2 * (wide - 1) + 16 + 4 * HALVES * (wide - 1) + 8
     any_spec = pl.BlockSpec(memory_space=pl.ANY)
+    hbm_spec = pl.BlockSpec(memory_space=pltpu.HBM)
     outs = pl.pallas_call(
         functools.partial(fused_kernel, wide),
         out_shape=(
@@ -527,7 +552,7 @@
             shape((K, D), f32), shape((K, D), f32), shape((K, D), f32),
             shape((K, CC), f32), shape((K, CC), f32), shape((K, CC), f32),
         ),
-        in_specs=[any_spec] * 9 + [pl.BlockSpec(memory_space=pltpu.SMEM), any_spec],
+        in_specs=[hbm_spec] * 11,
         out_specs=(any_spec,) * 8,
         scratch_shapes=[
             pltpu.VMEM((T, D), low), pltpu.VMEM((D, C), low), pltpu.VMEM((1, T), jnp.int32),
@@ -544,11 +569,12 @@
             pltpu.VMEM((wide, K, D), low), pltpu.VMEM((wide, K, D), low),
             pltpu.VMEM((8, 128), f32), pltpu.VMEM((T, D), low),
             pltpu.VMEM((A, CC), low), pltpu.VMEM((wide, K, CC), low), pltpu.VMEM((R, C), low),
+            pltpu.SMEM(rates.shape, f32),
             pltpu.SemaphoreType.DMA((20,)), pltpu.SemaphoreType.DMA((16 + 4 + 3 * HALVES,)),
             pltpu.SemaphoreType.DMA((remotes,)), pltpu.SemaphoreType.DMA((remotes,)),
         ],
         compiler_params=pltpu.CompilerParams(
-            collective_id=0, has_side_effects=True, vmem_limit_bytes=50 * 1024 * 1024
+            collective_id=0, has_side_effects=True, vmem_limit_bytes=64 * 1024 * 1024 - 65536
         ),
         cost_estimate=pl.CostEstimate(
             flops=2 * (2 * T * D * C + 3 * T * D * A), bytes_accessed=12 * 1024 * 1024, transcendentals=0
@@ -559,7 +585,14 @@
         down_moment_first.T, down_moment_second.T, up_moment_first, up_moment_second,
         rates, value_output_gradient,
     )
-    values, grad_tokens, dw, dm1, dm2, uw, um1, um2 = outs
+    values, grad_tokens, dw, dm1, dm2, uw, um1, um2 = pl.pallas_call(
+        write_kernel,
+        out_shape=tuple(shape(a.shape, a.dtype) for a in outs),
+        in_specs=[any_spec] * 8,
+        out_specs=(hbm_spec,) * 8,
+        scratch_shapes=[pltpu.VMEM(a.shape, a.dtype) for a in outs]
+        + [pltpu.SemaphoreType.DMA((11,)), pltpu.SemaphoreType.DMA((11,))],
+    )(*outs)
     return (values, grad_tokens, dw.T, dm1.T, dm2.T, uw, um1, um2)
 
 

time: 60.6 us -> 47.4 us (0.78)
  local copies, waits for them, and re-layouts: 15.2 us -> 0 us
  Pallas kernels: 44.2 us -> 46.6 us
    unnamed x26 -> x0, local copies, waits for them, and re-layouts: 15.2 us -> none
    pallas_call x0 -> x1, Pallas kernels: none -> 2.91 us  [fused_shards(): pl.pallas_call(write_kernel, out_shape=tuple((shape(a.shape, a.dtype) for...]
where the time goes in v2:
time: 47.4 us; the launch traced here: 47.3 us
  Pallas kernels  46.6 us (98%)
  between operations  0.65 us (1%)
    pallas_call x1, Pallas kernels, fused_shards(): pl.pallas_call(functools.partial(fused_kernel, wide), out_shape=(shape((R...  43.7 us
    pallas_call x1, Pallas kernels, fused_shards(): pl.pallas_call(write_kernel, out_shape=tuple((shape(a.shape, a.dtype) for...  2.91 us

profile of v2, /device:TPU:0, one launch (start us, length us, event | category | flops | bytes accessed | tf_op | source)
XLA Modules:
  0.0 47.3 jit_solution(3369775295676391437)
XLA Ops:
  0.6 43.7 %shard_map.170 = (bf16[128,1024]{1,0:T(8,128)(2,1)}, bf16[512,2048]{1,0:T(8,128)(2,1)}, f32[32,2048]{1,0:T(8,128)}, f32[32,2048]{1,0:T(8,128)}, f32[32,2048]{1,0...) custom-call(bf16[512,2048]{1,0:T(8,128)(2,1)} %tok_hbm.1, bf16[2048,1024]{1,0:T(8,128)(2,1)} %w_hbm.1, ...), custom_call_target="tpu_custom_call" | custom-call | flops 5100273664 | bytes 12582912 | tf_op jit(solution)/shard_map/pallas_call | solution.py:548
  44.4 2.9 %shard_map.171 = (bf16[128,1024]{1,0:T(8,128)(2,1)}, bf16[512,2048]{1,0:T(8,128)(2,1)}, f32[32,2048]{1,0:T(8,128)}, f32[32,2048]{1,0:T(8,128)}, f32[32,2048]{1,0...) custom-call(bf16[128,1024]{1,0:T(8,128)(2,1)} %get-tuple-element.24.refs_0_, ...), custom_call_target="tpu_custom_call" | custom-call | tf_op jit(solution)/shard_map/pallas_call | solution.py:588

commit v3 on v2

--- a/solution.py
+++ b/solution.py
@@ -223,7 +223,7 @@
     for m in (3, 1):
         load(("tok", m), tok_hbm.at[natural(block[m])], tok.at[rows(m)])
     for q in range(4):
-        load(("w", q), w_hbm.at[:, pl.ds(q * CC, CC)], w.at[:, pl.ds(q * CC, CC)])
+        load(("w", q), w_hbm.at[pl.ds(q * (D // 4), D // 4)], w.at[pl.ds(q * (D // 4), D // 4)])
     for m in (2, 0):
         load(("tok", m), tok_hbm.at[natural(block[m])], tok.at[rows(m)])
     for m in order:
@@ -294,14 +294,6 @@
         part = column(x * 2 + core)
         send(("g", m, 1), g.at[rows(0), part], g.at[rows(m), part], {"narrow": block[m]})
 
-    loads["tok", 3].wait()
-    loads["tok", 1].wait()
-    for q in range(4):
-        loads["w", q].wait()
-        cols = pl.ds(q * CC, CC)
-        psend[:, cols] = dot_nn(tok[0 : 2 * R, :], w[:, cols]).astype(jnp.bfloat16)
-    send("p", psend, precv, {"narrow": block[1]})
-
     for m in order:
         loads["idx", m].wait()
     adapter = lax.broadcasted_iota(jnp.int32, (A, T), 0) // ADAPTER_RANK
@@ -347,14 +339,17 @@
 
     down_step(1)
 
+    loads["tok", 3].wait()
+    loads["tok", 1].wait()
+    for q in range(4):
+        loads["w", q].wait()
+    for q in range(4):
+        cols = pl.ds(q * CC, CC)
+        psend[:, cols] = dot_nn(tok[0 : 2 * R, :], w[:, cols]).astype(jnp.bfloat16)
+    send("p", psend, precv, {"narrow": block[1]})
+
     loads["tok", 2].wait()
     loads["tok", 0].wait()
-    for q in range(4):
-        cols = pl.ds(q * CC, CC)
-        pacc[:, cols] = dot_nn(tok[2 * R :, :], w[:, cols])
-    arrived("p", precv)
-    xsend[...] = (pacc[0:R] + precv[0:R].astype(jnp.float32)).astype(jnp.bfloat16)
-    send("px", xsend, xrecv, {"narrow": block[2]})
 
     back = 2.0 * total_of("back", back_part, brecv, bnat)
     back_wide_t = spread_out(back)
@@ -391,8 +386,19 @@
                 rs_sent.append((ahead, copy))
 
     rs_step(0)
-    for s in range(2, wide):
+
+    for s in range(2, wide - 1):
         down_step(s)
+
+    for q in range(4):
+        cols = pl.ds(q * CC, CC)
+        pacc[:, cols] = dot_nn(tok[2 * R :, :], w[:, cols])
+    arrived("p", precv)
+    xsend[...] = (pacc[0:R] + precv[0:R].astype(jnp.float32)).astype(jnp.bfloat16)
+    send("px", xsend, xrecv, {"narrow": block[2]})
+
+    if wide > 2:
+        down_step(wide - 1)
 
     for m, to in ((2, 3), (3, 2)):
         part = column(xo * 2 + c)
@@ -404,6 +410,8 @@
 
     code_part = pack(dot_nt(tok[...], downf[...]).T)
     exchange("code", code_part, csend, crecv)
+    if wide > 2:
+        rs_step(1)
 
     for m in (2, 3):
         arrived(("g_fwd", 5 - m, 0), g.at[rows(m), column(block[1])])
@@ -418,8 +426,6 @@
             store(gt.at[rows(m), span], gt_out.at[natural(block[m]), span])
 
     grad_tokens(0, 4)
-    if wide > 2:
-        rs_step(1)
 
     code = total_of("code", code_part, crecv, cnat)
     code_wide_t = spread_out(code)
@@ -429,9 +435,9 @@
         to = lax.rem(z + d, wide)
         send(("gu", d), gu_stage.at[shard(to)], gu_recv.at[d], {"wide": to})
 
-    grad_tokens(1, 4)
     for k in range(2, wide - 1):
         rs_step(k)
+    grad_tokens(1, 4)
     grad_tokens(2, 4)
     grad_tokens(3, 4)
 

time: 47.4 us -> 46 us (0.970)
  Pallas kernels: 46.6 us -> 45.2 us
    pallas_call x1, Pallas kernels: 43.7 us -> 42.3 us  [fused_shards(): pl.pallas_call(functools.partial(fused_kernel, wide), out_shape=(shape((R...]
where the time goes in v3:
time: 46 us; the launch traced here: 45.8 us
  Pallas kernels  45.2 us (98%)
  between operations  0.65 us (1%)
    pallas_call x1, Pallas kernels, fused_shards(): pl.pallas_call(functools.partial(fused_kernel, wide), out_shape=(shape((R...  42.3 us
    pallas_call x1, Pallas kernels, fused_shards(): pl.pallas_call(write_kernel, out_shape=tuple((shape(a.shape, a.dtype) for...  2.91 us

profile of v3, /device:TPU:0, one launch (start us, length us, event | category | flops | bytes accessed | tf_op | source)
XLA Modules:
  0.0 45.8 jit_solution(3091753459890416173)
XLA Ops:
  0.6 42.3 %shard_map.170 = (bf16[128,1024]{1,0:T(8,128)(2,1)}, bf16[512,2048]{1,0:T(8,128)(2,1)}, f32[32,2048]{1,0:T(8,128)}, f32[32,2048]{1,0:T(8,128)}, f32[32,2048]{1,0...) custom-call(bf16[512,2048]{1,0:T(8,128)(2,1)} %tok_hbm.1, bf16[2048,1024]{1,0:T(8,128)(2,1)} %w_hbm.1, ...), custom_call_target="tpu_custom_call" | custom-call | flops 5100273664 | bytes 12582912 | tf_op jit(solution)/shard_map/pallas_call | solution.py:554
  42.9 2.9 %shard_map.171 = (bf16[128,1024]{1,0:T(8,128)(2,1)}, bf16[512,2048]{1,0:T(8,128)(2,1)}, f32[32,2048]{1,0:T(8,128)}, f32[32,2048]{1,0:T(8,128)}, f32[32,2048]{1,0...) custom-call(bf16[128,1024]{1,0:T(8,128)(2,1)} %get-tuple-element.24.refs_0_, ...), custom_call_target="tpu_custom_call" | custom-call | tf_op jit(solution)/shard_map/pallas_call | solution.py:594
